TPU v7x, 32 devices: a whole 2x2x4 slice. The times are simulated.
32 devices in a mesh: fsdp: 8 (over z, x), ctx: 2 (over y), tp: 2 (over core).
Axes of the slice: x: 2, y: 2, z: 4, core: 2. Of those that a mesh axis runs over, the one named last changes fastest.
Arguments:
- latents_in: float32 [32, 1024, 384], P('fsdp', 'ctx'), may hold values from -6 to 6
- condition: float32 [32, 384], P('fsdp'), may hold values from -6 to 6
- w_mod: bfloat16 [384, 6, 384], P('fsdp', 'tp'), may hold values from -0.3125 to 0.3125
- b_mod: bfloat16 [6, 384], P('tp', 'fsdp'), may hold values from -3 to 3
- w_qkv: bfloat16 [384, 3, 384], P('fsdp', None, 'tp'), may hold values from -0.3125 to 0.3125
- b_qv: bfloat16 [2, 384], P(None, ('tp', 'fsdp')), may hold values from -3 to 3
- w_out: bfloat16 [384, 384], P('tp', 'fsdp'), may hold values from -3 to 3
- b_out: bfloat16 [384], P('fsdp'), may hold values from -3 to 3
- up_weight: bfloat16 [384, 1536], P('fsdp', 'tp'), may hold values from -0.3125 to 0.3125
- up_projection_bias: bfloat16 [1536], P(('tp', 'fsdp')), may hold values from -3 to 3
- down_weight: bfloat16 [1536, 384], P('tp', 'fsdp'), may hold values from -0.15625 to 0.15625
- down_projection_bias: bfloat16 [384], P('fsdp'), may hold values from -3 to 3
- cotangent: float32 [32, 1024, 384], P('fsdp', 'ctx'), may hold values from -6 to 6
Outputs:
- block_out: float32 [32, 1024, 384], P('fsdp', 'ctx')
- latents_grad: float32 [32, 1024, 384], P('fsdp', 'ctx')
- condition_grad: float32 [32, 384], P('fsdp')
- w_mod_grad: float32 [384, 6, 384], P('fsdp', 'tp')
- b_mod_grad: float32 [6, 384], P('tp', 'fsdp')
- w_qkv_grad: float32 [384, 3, 384], P('fsdp', None, 'tp')
- b_qv_grad: float32 [2, 384], P(None, ('tp', 'fsdp'))
- w_out_grad: float32 [384, 384], P('tp', 'fsdp')
- b_out_grad: float32 [384], P('fsdp')
- w_up_grad: float32 [384, 1536], P('fsdp', 'tp')
- b_up_grad: float32 [1536], P(('tp', 'fsdp'))
- w_down_grad: float32 [1536, 384], P('tp', 'fsdp')
- b_down_grad: float32 [384], P('fsdp')
All inputs are finite; a program needn't handle non-finite values.
Results may differ from a plain program's by a relative error of at most 0.013.
The roundings to bfloat16 on the way count: a program that leaves them out, or rounds other values in their place, can miss the bound.
Values may be sent and summed in bfloat16 or wider, within the bound.
A program may use at most 128 MiB of HBM per device.

v0:
```python
import math

import jax
import jax.numpy as jnp
from jax import lax
from jax.sharding import PartitionSpec as P

HD = 64


EPSILON = 1e-06


def normalize(values):
    centre = values - jnp.mean(values, axis=-1, keepdims=True)
    inverse = lax.rsqrt(jnp.mean(centre * centre, axis=-1, keepdims=True) + EPSILON)
    return (centre * inverse, inverse)


def norm_back(upstream, normed, inverse):
    return inverse * (
        upstream
        - jnp.mean(upstream, axis=-1, keepdims=True)
        - normed * jnp.mean(upstream * normed, axis=-1, keepdims=True)
    )


def attend_forward(blocks):
    query_rows, key_rows, value_rows = blocks
    factor = 1.0 / math.sqrt(HD)
    scores = (
        jnp.einsum("qhc,khc->hqk", query_rows, key_rows, preferred_element_type=jnp.float32)
        * factor
    )
    highest = jnp.max(scores, axis=-1, keepdims=True)
    exponent = jnp.exp(scores - highest)
    totals = jnp.sum(exponent, axis=-1, keepdims=True)
    softmax_rows = (exponent / totals).astype(jnp.bfloat16)
    mixed_rows = jnp.einsum(
        "hqk,khc->qhc", softmax_rows, value_rows, preferred_element_type=jnp.float32
    )
    return (mixed_rows.astype(jnp.bfloat16), (highest + jnp.log(totals))[..., 0])


def attend_backward(blocks):
    query_rows, key_rows, value_rows, attended_grad, log_totals = blocks
    factor = 1.0 / math.sqrt(HD)
    scores = (
        jnp.einsum("qhc,khc->hqk", query_rows, key_rows, preferred_element_type=jnp.float32)
        * factor
    )
    softmax_rows = jnp.exp(scores - log_totals[..., None])
    prob_grad = jnp.einsum(
        "qhc,khc->hqk", attended_grad, value_rows, preferred_element_type=jnp.float32
    )
    row_inner = jnp.sum(prob_grad * softmax_rows, axis=-1, keepdims=True)
    score_grad = (softmax_rows * (prob_grad - row_inner)).astype(jnp.bfloat16)
    query_grad = (
        jnp.einsum("hqk,khc->qhc", score_grad, key_rows, preferred_element_type=jnp.float32)
        * factor
    ).astype(jnp.bfloat16)
    key_grad = (
        jnp.einsum("hqk,qhc->khc", score_grad, query_rows, preferred_element_type=jnp.float32)
        * factor
    )
    value_grad = jnp.einsum(
        "hqk,qhc->khc",
        softmax_rows.astype(jnp.bfloat16),
        attended_grad,
        preferred_element_type=jnp.float32,
    )
    return (query_grad, key_grad, value_grad)


def shards(
    latents_in,
    condition,
    w_mod,
    b_mod,
    w_qkv,
    b_qv,
    w_out,
    b_out,
    up_weight,
    up_projection_bias,
    down_weight,
    down_projection_bias,
    cotangent,
):
    (
        mod_full,
        mod_bias,
        qkv_full,
        qv_bias,
        out_full,
        out_bias,
        up_weight_gathered,
        up_bias_vector,
        down_weight_gathered,
        down_bias,
    ) = (
        lax.all_gather(w_mod, "fsdp", axis=0, tiled=True),
        lax.all_gather(b_mod, "fsdp", axis=1, tiled=True),
        lax.all_gather(w_qkv, "fsdp", axis=0, tiled=True),
        lax.all_gather(b_qv, "fsdp", axis=1, tiled=True),
        lax.all_gather(w_out, "fsdp", axis=1, tiled=True),
        lax.all_gather(b_out, "fsdp", axis=0, tiled=True),
        lax.all_gather(up_weight, "fsdp", axis=0, tiled=True),
        lax.all_gather(up_projection_bias, "fsdp", axis=0, tiled=True),
        lax.all_gather(down_weight, "fsdp", axis=1, tiled=True),
        lax.all_gather(down_projection_bias, "fsdp", axis=0, tiled=True),
    )
    latent_count = latents_in.shape[0]
    token_count = latents_in.shape[1]
    local_width = qkv_full.shape[2]
    heads_here = local_width // HD
    own_stretches = mod_full.shape[1]
    silu_cond = jax.nn.silu(condition).astype(jnp.bfloat16)
    own_mod = (
        jnp.einsum("ld,dkc->lkc", silu_cond, mod_full, preferred_element_type=jnp.float32)
        + mod_bias
    )
    modulation = lax.all_gather(own_mod, "tp", axis=1, tiled=True)
    shift_one = modulation[:, 0][:, None, :]
    scale_one = modulation[:, 1][:, None, :]
    gate_one = modulation[:, 2][:, None, :]
    shift_two = modulation[:, 3][:, None, :]
    scale_two = modulation[:, 4][:, None, :]
    gate_two = modulation[:, 5][:, None, :]
    normed_one, inverse_one = normalize(latents_in)
    hidden_one = (normed_one * (1.0 + scale_one) + shift_one).astype(jnp.bfloat16)
    projected = jnp.einsum(
        "lsd,dkc->lskc", hidden_one, qkv_full, preferred_element_type=jnp.float32
    )
    query_rows = (projected[:, :, 0] + qv_bias[0]).astype(jnp.bfloat16)
    key_rows = projected[:, :, 1].astype(jnp.bfloat16)
    value_rows = (projected[:, :, 2] + qv_bias[1]).astype(jnp.bfloat16)
    key_all, value_all = (
        lax.all_gather(key_rows, "ctx", axis=1, tiled=True),
        lax.all_gather(value_rows, "ctx", axis=1, tiled=True),
    )

    def split_heads(rows):
        return rows.reshape(rows.shape[0], rows.shape[1], heads_here, HD)

    query_heads = split_heads(query_rows)
    key_heads = split_heads(key_all)
    value_heads = split_heads(value_all)
    attended, log_totals = lax.map(attend_forward, (query_heads, key_heads, value_heads))
    attended = attended.reshape(latent_count, token_count, local_width)
    branch = (
        lax.psum(
            jnp.einsum("lsc,cd->lsd", attended, out_full, preferred_element_type=jnp.float32), "tp"
        )
        + out_bias
    )
    middle = latents_in + gate_one * branch
    normed_two, inverse_two = normalize(middle)
    second_hidden_state = (normed_two * (1.0 + scale_two) + shift_two).astype(jnp.bfloat16)
    up_projection_input = (
        jnp.einsum(
            "vae,et->vat",
            second_hidden_state,
            up_weight_gathered,
            preferred_element_type=jnp.float32,
        )
        + up_bias_vector
    )
    activation_value = jax.nn.gelu(up_projection_input, approximate=True).astype(jnp.bfloat16)
    feedforward_output = (
        lax.psum(
            jnp.einsum(
                "vmr,rh->vmh",
                activation_value,
                down_weight_gathered,
                preferred_element_type=jnp.float32,
            ).astype(jnp.bfloat16),
            "tp",
        ).astype(jnp.float32)
        + down_bias
    )
    block_out = middle + gate_two * feedforward_output
    gate_two_grad = jnp.sum(cotangent * feedforward_output, axis=1)
    down_projection_input = (cotangent * gate_two).astype(jnp.bfloat16)
    down_bias_grad = jnp.sum(down_projection_input, axis=(0, 1), dtype=jnp.float32)
    down_weight_grad = jnp.einsum(
        "rit,riy->ty", activation_value, down_projection_input, preferred_element_type=jnp.float32
    )
    activation_gradient = jnp.einsum(
        "uqe,ye->uqy",
        down_projection_input,
        down_weight_gathered,
        preferred_element_type=jnp.float32,
    )
    gelu_value, gelu_pull = jax.vjp(
        lambda upper_rows: jax.nn.gelu(upper_rows, approximate=True), up_projection_input
    )
    up_projection_gradient = gelu_pull(activation_gradient)[0].astype(jnp.bfloat16)
    up_bias_grad = jnp.sum(up_projection_gradient, axis=(0, 1), dtype=jnp.float32)
    up_weight_grad = jnp.einsum(
        "jnv,jnz->vz",
        second_hidden_state,
        up_projection_gradient,
        preferred_element_type=jnp.float32,
    )
    hidden_two_grad = lax.psum(
        jnp.einsum(
            "jam,em->jae",
            up_projection_gradient,
            up_weight_gathered,
            preferred_element_type=jnp.float32,
        ),
        "tp",
    )
    scale_two_grad = jnp.sum(hidden_two_grad * normed_two, axis=1)
    shift_two_grad = jnp.sum(hidden_two_grad, axis=1)
    middle_grad = cotangent + norm_back(
        hidden_two_grad * (1.0 + scale_two), normed_two, inverse_two
    )
    gate_one_grad = jnp.sum(middle_grad * branch, axis=1)
    branch_grad = (middle_grad * gate_one).astype(jnp.bfloat16)
    out_bias_grad = jnp.sum(branch_grad, axis=(0, 1), dtype=jnp.float32)
    out_weight_grad = jnp.einsum(
        "lsc,lsd->cd", attended, branch_grad, preferred_element_type=jnp.float32
    )
    attended_grad = jnp.einsum(
        "lsd,cd->lsc", branch_grad, out_full, preferred_element_type=jnp.float32
    ).astype(jnp.bfloat16)
    attended_heads = split_heads(attended_grad)
    query_grad, key_grad, value_grad = lax.map(
        attend_backward, (query_heads, key_heads, value_heads, attended_heads, log_totals)
    )
    key_grad = key_grad.reshape(latent_count, key_all.shape[1], local_width)
    value_grad = value_grad.reshape(latent_count, key_all.shape[1], local_width)
    key_grad, value_grad = (
        lax.psum_scatter(key_grad, "ctx", scatter_dimension=1, tiled=True),
        lax.psum_scatter(value_grad, "ctx", scatter_dimension=1, tiled=True),
    )
    key_grad = key_grad.astype(jnp.bfloat16)
    value_grad = value_grad.astype(jnp.bfloat16)
    query_grad = query_grad.reshape(latent_count, token_count, local_width)
    qv_bias_grad = jnp.stack(
        [
            jnp.sum(query_grad, axis=(0, 1), dtype=jnp.float32),
            jnp.sum(value_grad, axis=(0, 1), dtype=jnp.float32),
        ]
    )
    projected_grad = jnp.stack([query_grad, key_grad, value_grad], axis=2)
    qkv_weight_grad = jnp.einsum(
        "lsd,lskc->dkc", hidden_one, projected_grad, preferred_element_type=jnp.float32
    )
    hidden_one_grad = lax.psum(
        jnp.einsum(
            "lskc,dkc->lsd", projected_grad, qkv_full, preferred_element_type=jnp.float32
        ).astype(jnp.bfloat16),
        "tp",
    ).astype(jnp.float32)
    scale_one_grad = jnp.sum(hidden_one_grad * normed_one, axis=1)
    shift_one_grad = jnp.sum(hidden_one_grad, axis=1)
    latents_grad = middle_grad + norm_back(
        hidden_one_grad * (1.0 + scale_one), normed_one, inverse_one
    )
    modulation_grad = jnp.stack(
        [
            shift_one_grad,
            scale_one_grad,
            gate_one_grad,
            shift_two_grad,
            scale_two_grad,
            gate_two_grad,
        ],
        axis=1,
    )
    own_grad = lax.dynamic_slice_in_dim(
        modulation_grad, lax.axis_index("tp") * own_stretches, own_stretches, axis=1
    )
    mod_weight_grad = jnp.einsum(
        "ld,lkc->dkc", silu_cond.astype(jnp.float32), own_grad, precision=lax.Precision.HIGHEST
    )
    mod_bias_grad = jnp.sum(own_grad, axis=0)
    silu_term = jnp.einsum(
        "lkc,dkc->ld", own_grad, mod_full.astype(jnp.float32), precision=lax.Precision.HIGHEST
    )
    silu_total = lax.psum(silu_term, ("ctx", "tp"))
    silu_value, silu_pull = jax.vjp(jax.nn.silu, condition)
    condition_grad = silu_pull(silu_total)[0]
    full_grads = (
        mod_weight_grad,
        mod_bias_grad,
        qkv_weight_grad,
        qv_bias_grad,
        out_weight_grad,
        out_bias_grad,
        up_weight_grad,
        up_bias_grad,
        down_weight_grad,
        down_bias_grad,
    )
    summed = (
        lax.psum(full_grads[0].astype(jnp.bfloat16), "ctx").astype(jnp.float32),
        lax.psum(full_grads[1].astype(jnp.bfloat16), "ctx").astype(jnp.float32),
        lax.psum(full_grads[2].astype(jnp.bfloat16), "ctx").astype(jnp.float32),
        lax.psum(full_grads[3].astype(jnp.bfloat16), "ctx").astype(jnp.float32),
        lax.psum(full_grads[4].astype(jnp.bfloat16), "ctx").astype(jnp.float32),
        lax.psum(full_grads[5].astype(jnp.bfloat16), "ctx").astype(jnp.float32),
        lax.psum(full_grads[6].astype(jnp.bfloat16), "ctx").astype(jnp.float32),
        lax.psum(full_grads[7].astype(jnp.bfloat16), "ctx").astype(jnp.float32),
        lax.psum(full_grads[8].astype(jnp.bfloat16), "ctx").astype(jnp.float32),
        lax.psum(full_grads[9].astype(jnp.bfloat16), "ctx").astype(jnp.float32),
    )
    owned = (
        lax.psum_scatter(summed[0], "fsdp", scatter_dimension=0, tiled=True),
        lax.psum_scatter(summed[1], "fsdp", scatter_dimension=1, tiled=True),
        lax.psum_scatter(summed[2], "fsdp", scatter_dimension=0, tiled=True),
        lax.psum_scatter(summed[3], "fsdp", scatter_dimension=1, tiled=True),
        lax.psum_scatter(summed[4], "fsdp", scatter_dimension=1, tiled=True),
        lax.psum_scatter(summed[5], "fsdp", scatter_dimension=0, tiled=True),
        lax.psum_scatter(summed[6], "fsdp", scatter_dimension=0, tiled=True),
        lax.psum_scatter(summed[7], "fsdp", scatter_dimension=0, tiled=True),
        lax.psum_scatter(summed[8], "fsdp", scatter_dimension=1, tiled=True),
        lax.psum_scatter(summed[9], "fsdp", scatter_dimension=0, tiled=True),
    )
    return (
        block_out,
        latents_grad,
        condition_grad,
        owned[0],
        owned[1],
        owned[2],
        owned[3],
        owned[4],
        owned[5],
        owned[6],
        owned[7],
        owned[8],
        owned[9],
    )


def solution(mesh):
    placed = (
        P("fsdp", "ctx", None),
        P("fsdp", None),
        P("fsdp", "tp", None),
        P("tp", "fsdp"),
        P("fsdp", None, "tp"),
        P(None, ("tp", "fsdp")),
        P("tp", "fsdp"),
        P("fsdp"),
        P("fsdp", "tp"),
        P(("tp", "fsdp")),
        P("tp", "fsdp"),
        P("fsdp"),
        P("fsdp", "ctx", None),
    )
    return jax.shard_map(
        shards,
        mesh=mesh,
        in_specs=placed,
        out_specs=(
            P("fsdp", "ctx", None),
            P("fsdp", "ctx", None),
            P("fsdp", None),
            P("fsdp", "tp", None),
            P("tp", "fsdp"),
            P("fsdp", None, "tp"),
            P(None, ("tp", "fsdp")),
            P("tp", "fsdp"),
            P("fsdp"),
            P("fsdp", "tp"),
            P(("tp", "fsdp")),
            P("tp", "fsdp"),
            P("fsdp"),
        ),
        check_vma=False,
    )
```

profile of v0, /device:TPU:0, one launch (start us, length us, event | category | flops | bytes accessed | tf_op | source)
XLA Modules:
  0.0 1041.2 jit_solution(11101993983332344698)
XLA Ops:
  7.2 22.4 %all-gather.2 = bf16[8,24,2]{1,2,0:T(2,128)(2,1)S(1)} all-gather(bf16[1,24,2]{1,2,0:T(2,128)(2,1)} %bitcast.253), channel_id=1, replica_groups=mesh['fsdp'=8,'ctx'=2,'tp'=2] {'fsdp'}, dimensions={0}, use_global_device_ids=true | all-gather | bytes 864 | tf_op jit(solution)/shard_map/all_gather | solution.py:105
  29.8 16.6 %all-gather.1 = bf16[8,48,3]{1,2,0:T(4,128)(2,1)S(1)} all-gather(bf16[1,48,3]{1,2,0:T(4,128)(2,1)} %bitcast.252), channel_id=1, replica_groups=mesh['fsdp'=8,'ctx'=2,'tp'=2] {'fsdp'}, dimensions={0}, use_global_device_ids=true | all-gather | bytes 2592 | tf_op jit(solution)/shard_map/all_gather | solution.py:103
  49.5 31.8 %all_gather.42 = bf16[384,3,192]{2,0,1:T(8,128)(2,1)S(1)} all-gather(bf16[48,3,192]{2,0,1:T(8,128)(2,1)S(1)} %copy-done.37), channel_id=1, replica_groups=mesh['fsdp'=8,'ctx'=2,'tp'=2] {'fsdp'}, dimensions={0}, use_global_device_ids=true | all-gather | bytes 497664 | tf_op jit(solution)/shard_map/all_gather | solution.py:104
  81.3 32.0 %all_gather.39 = bf16[384,3,384]{2,0,1:T(8,128)(2,1)S(1)} all-gather(bf16[48,3,384]{2,0,1:T(8,128)(2,1)S(1)} %copy-done.34), channel_id=1, replica_groups=mesh['fsdp'=8,'ctx'=2,'tp'=2] {'fsdp'}, dimensions={0}, use_global_device_ids=true | all-gather | bytes 995328 | tf_op jit(solution)/shard_map/all_gather | solution.py:102
  126.8 30.7 %all_gather.46 = bf16[192,384]{0,1:T(8,128)(2,1)S(1)} all-gather(bf16[192,48]{0,1:T(8,128)(2,1)S(1)} %copy-done.44), channel_id=1, replica_groups=mesh['fsdp'=8,'ctx'=2,'tp'=2] {'fsdp'}, dimensions={1}, use_global_device_ids=true | all-gather | bytes 165888 | tf_op jit(solution)/shard_map/all_gather | solution.py:106
  160.1 16.1 %all-gather.8.cloned.1.call-done = bf16[4,1024,1,192]{1,3,2,0:T(8,128)(2,1)} async-done(((bf16[4,512,1,192]{1,3,2,0:T(8,128)(2,1)}), bf16[4,1024,1,192]{1,3,2,0:T(8,128)(2,1)}) %all-gather.8.cloned.1.call-update) | async-done | bytes 1572880 | tf_op jit(solution)/shard_map/all_gather | solution.py:139
  177.1 28.1 %while.26 = (s32[]{:T(128)}, bf16[4,512,3,64]{1,3,2,0:T(8,128)(2,1)}, f32[4,3,512]{2,1,0:T(4,128)S(1)}, bf16[4,1024,3,64]{1,3,2,0:T(8,128)(2,1)}, bf16[4,512,3,6...) while((s32[]{:T(128)}, bf16[4,512,3,64]{1,3,2,0:T(8,128)(2,1)}, ...), condition=%wide.region_5.6_spmd, body=%wide.region_2.5_spmd.sunk | while | flops 416905728 | bytes 20111448 | solution.py:149
  180.6 3.5 fusion.141
  187.7 3.5 fusion.141
  194.7 3.5 fusion.141
  201.7 3.5 fusion.141
  205.3 3.6 fusion.85
  215.0 22.0 %all-reduce.8 = (bf16[384]{0:T(512)(128)(2,1)S(1)}, bf16[768]{0:T(1024)(128)(2,1)}, bf16[384]{0:T(512)(128)(2,1)}) all-reduce(bf16[384]{0:T(512)(128)(2,1)} %dynamic-update-slice, bf16[768]{0:T(1024)(128)(2,1)S(1)} %dynamic-update-slice.1, bf16[384]{0:T(512)(128)(2,1)} %copy-done.49), channel_id=1, replica_groups=mesh['fsdp'=8,'ctx'=2,'tp'=2] {'fsdp'}, use_global_device_ids=true, to_apply=%add | all-reduce | flops 1536 | bytes 6144
  237.7 33.6 %all_gather.48 = bf16[384,768]{1,0:T(8,128)(2,1)} all-gather(bf16[48,768]{1,0:T(8,128)(2,1)S(1)} %copy-done.38), channel_id=1, replica_groups=mesh['fsdp'=8,'ctx'=2,'tp'=2] {'fsdp'}, dimensions={0}, use_global_device_ids=true | all-gather | bytes 663552 | tf_op jit(solution)/shard_map/all_gather | solution.py:108
  271.4 33.7 %all_gather.50 = bf16[768,384]{0,1:T(8,128)(2,1)} all-gather(bf16[768,48]{0,1:T(8,128)(2,1)S(1)} %copy-done.39), channel_id=1, replica_groups=mesh['fsdp'=8,'ctx'=2,'tp'=2] {'fsdp'}, dimensions={1}, use_global_device_ids=true | all-gather | bytes 663552 | tf_op jit(solution)/shard_map/all_gather | solution.py:110
  305.0 4.0 fusion.105
  313.0 4.5 multiply_convert_fusion.1
  317.5 5.3 fusion.109
  324.5 3.5 fusion.77
  328.3 19.4 %all-reduce.19.cloned.1.call-done = f32[4,512,384]{2,1,0:T(8,128)} async-done(((f32[4,512,384]{2,1,0:T(8,128)}), f32[4,512,384]{2,1,0:T(8,128)}) %all-reduce.19.cloned.1.call-update) | async-done | bytes 3145744 | tf_op jit(solution)/shard_map/psum | solution.py:206
  347.7 4.1 multiply_reduce_fusion.3
  352.5 5.2 fusion.106
  361.5 56.4 %while.27 = (s32[]{:T(128)}, bf16[4,512,3,64]{1,3,2,0:T(8,128)(2,1)}, f32[4,1024,3,64]{1,3,2,0:T(8,128)}, f32[4,1024,3,64]{1,3,2,0:T(8,128)}, bf16[4,1024,3,64]{...) while((s32[]{:T(128)}, ...), condition=%wide.region_15.16_spmd, body=%wide.region_13.15_spmd.sunk | while | flops 1025899008 | bytes 54119564 | solution.py:230
  365.9 2.9 multiply_reduce_fusion.12
  370.3 2.8 fusion.151
  379.9 2.9 multiply_reduce_fusion.12
  394.0 2.9 multiply_reduce_fusion.12
  408.1 2.9 multiply_reduce_fusion.12
  418.5 5.0 convolution_convert_fusion
  423.5 39.1 %reduce-scatter.12.cloned.1.call-done = f32[4,512,192]{1,2,0:T(8,128)} async-done(((f32[4,1024,192]{1,2,0:T(8,128)}), f32[4,512,192]{1,2,0:T(8,128)}) %reduce-scatter.12.cloned.1.call-update) | async-done | bytes 1572880 | tf_op jit(solution)/shard_map/reduce_scatter | solution.py:236
  465.0 43.1 %reduce-scatter.14.cloned.1.call-done = f32[4,512,192]{1,2,0:T(8,128)} async-done(((f32[4,1024,192]{1,2,0:T(8,128)}), f32[4,512,192]{1,2,0:T(8,128)}) %reduce-scatter.14.cloned.1.call-update) | async-done | bytes 1572880 | tf_op jit(solution)/shard_map/reduce_scatter | solution.py:237
  510.5 4.6 bitcast_convert_fusion
  515.8 4.8 fusion.73
  524.8 2.9 fusion.71
  527.7 10.8 %all-reduce.21.cloned.1.call-done = (bf16[4,512,384]{2,1,0:T(8,128)(2,1)}, bf16[4,512,384]{2,1,0:T(8,128)(2,1)}) async-done(((bf16[4,512,384]{2,1,0:T(8,128)(2,1)}, bf16[4,512,384]{2,1,0:T(8,128)(2,1)}), (bf16[4,512,384]{2,1,0:T(8,128)(2,1)}, bf16[4,512,384]{2,1,0:T(8,128)(2,1)})) %all-reduce.21.cloned.1.call-update) | async-done | bytes 3145744 | tf_op jit(solution)/shard_map/psum | solution.py:171
  538.5 3.0 fusion.67
  541.6 4.5 multiply_reduce_fusion.2
  546.7 2.9 multiply_reduce_fusion.4
  552.1 5.0 all-reduce.10
  558.1 74.9 %all-reduce.23.cloned.1.call-done = (bf16[384,3,384]{2,0,1:T(8,128)(2,1)}, bf16[384,3,192]{2,0,1:T(8,128)(2,1)}, bf16[192,384]{0,1:T(8,128)(2,1)}, bf16[384,768]{1,0:T(8,128)(2,1)}, bf16[768,384]{0,1:T(8,128)(2,1)}) async-done(((bf16[384,3,384]{2,0,1:T(8,128)(2,1)}, bf16[384,3,192]{2,0,1:T(8,128)(2,1)}, bf16[192,384]{0,1:T(8,128)(2,1)}, bf16[384,768]{1,0:T(8,128)(2,1)}, bf16[768,384]{0,1:T(8,128)(2,1)}), ...) | async-done | bytes 2654224 | tf_op jit(solution)/shard_map/psum | solution.py:300
  642.8 37.1 %all-reduce.7 = (f32[2,192]{1,0:T(2,128)S(1)}, f32[384]{0:T(512)S(1)}, f32[768]{0:T(1024)S(1)}, f32[384]{0:T(512)S(1)}) all-reduce(bf16[2,192]{1,0:T(2,128)(2,1)S(1)} %get-tuple-element.148, bf16[384]{0:T(512)(128)(2,1)S(1)} %get-tuple-element.149, ...), channel_id=8, replica_groups=mesh['fsdp'=8,'ctx'=2,'tp'=2] {'fsdp'}, use_global_device_ids=true, to_apply=%region_38.39.clone | all-reduce | flops 1920 | bytes 11520
  682.5 6.0 psum.109
  689.7 7.9 reduce-scatter.26.cloned.1.call-done
  699.0 63.2 %reduce-scatter.20.cloned.1.call-done = f32[192,48]{0,1:T(8,128)} async-done(((f32[192,384]{0,1:T(8,128)}), f32[192,48]{0,1:T(8,128)}) %reduce-scatter.20.cloned.1.call-update) | async-done | bytes 36880 | tf_op jit(solution)/shard_map/reduce_scatter | solution.py:316
  762.2 67.3 %reduce-scatter.18.cloned.1.call-done = f32[48,3,192]{2,0,1:T(8,128)} async-done(((f32[384,3,192]{2,0,1:T(8,128)}), f32[48,3,192]{2,0,1:T(8,128)}) %reduce-scatter.18.cloned.1.call-update) | async-done | bytes 110608 | tf_op jit(solution)/shard_map/reduce_scatter | solution.py:314
  829.5 67.2 %reduce-scatter.22.cloned.1.call-done = f32[48,768]{1,0:T(8,128)} async-done(((f32[384,768]{1,0:T(8,128)}), f32[48,768]{1,0:T(8,128)}) %reduce-scatter.22.cloned.1.call-update) | async-done | bytes 147472 | tf_op jit(solution)/shard_map/reduce_scatter | solution.py:318
  896.8 67.3 %reduce-scatter.24.cloned.1.call-done = f32[768,48]{0,1:T(8,128)} async-done(((f32[768,384]{0,1:T(8,128)}), f32[768,48]{0,1:T(8,128)}) %reduce-scatter.24.cloned.1.call-update) | async-done | bytes 147472 | tf_op jit(solution)/shard_map/reduce_scatter | solution.py:320
  964.1 70.1 %reduce-scatter.16.cloned.1.call-done = f32[48,3,384]{2,0,1:T(8,128)} async-done(((f32[384,3,384]{2,0,1:T(8,128)}), f32[48,3,384]{2,0,1:T(8,128)}) %reduce-scatter.16.cloned.1.call-update) | async-done | bytes 221200 | tf_op jit(solution)/shard_map/reduce_scatter | solution.py:312
  (249 shorter events, 119.1 us)
Async XLA Ops:
  7.2 41.6 %copy-start = (f32[4,512,384]{2,1,0:T(8,128)S(1)}, f32[4,512,384]{2,1,0:T(8,128)}, u32[]{:S(2)}) copy-start(f32[4,512,384]{2,1,0:T(8,128)} %param.17) | copy-start | bytes 9437188
  7.2 152.9 %all-gather.6.cloned.1.call-start = ((), (), s32[]{:S(2)}) async-start(), calls=%async_computation.8 | async-start | bytes 2359296 | tf_op jit(solution)/shard_map/all_gather | solution.py:140
  46.4 3.0 copy-start.37
  46.4 34.8 %copy-start.34 = (bf16[48,3,384]{2,0,1:T(8,128)(2,1)S(1)}, bf16[48,3,384]{2,0,1:T(8,128)(2,1)}, u32[]{:S(2)}) copy-start(bf16[48,3,384]{2,0,1:T(8,128)(2,1)} %param.19) | copy-start | bytes 331780
  48.7 64.6 %copy-start.40 = (f32[4,384]{1,0:T(4,128)S(1)}, f32[4,384]{1,0:T(4,128)}, u32[]{:S(2)}) copy-start(f32[4,384]{1,0:T(4,128)} %param.18) | copy-start | bytes 18436
  48.8 69.5 %copy-start.30 = (f32[4,512]{1,0:T(4,128)}, f32[4,512]{1,0:T(4,128)S(1)}, u32[]{:S(2)}) copy-start(f32[4,512]{1,0:T(4,128)S(1)} %broadcast_multiply_fusion.5) | copy-start | bytes 24580
  49.5 68.8 %copy-start.32 = (f32[4,512]{1,0:T(4,128)}, f32[4,512]{1,0:T(4,128)S(1)}, u32[]{:S(2)}) copy-start(f32[4,512]{1,0:T(4,128)S(1)} %add_rsqrt_fusion.1) | copy-start | bytes 24580
  81.3 37.0 %copy-start.19 = (bf16[384,3,192]{2,0,1:T(8,128)(2,1)}, bf16[384,3,192]{2,0,1:T(8,128)(2,1)S(1)}, u32[]{:S(2)}) copy-start(bf16[384,3,192]{2,0,1:T(8,128)(2,1)S(1)} %all_gather.42) | copy-start | bytes 1327108
  121.5 5.3 copy-start.44
  121.5 54.7 %all-gather.8.cloned.1.call-start = ((), (), s32[]{:S(2)}) async-start(), calls=%async_computation.18 | async-start | bytes 2359296 | tf_op jit(solution)/shard_map/all_gather | solution.py:139
  124.0 185.1 %all-reduce.17.cloned.1.call-start = ((), (), s32[]{:S(2)}) async-start(), calls=%async_computation.9 | async-start | bytes 6291456 | tf_op jit(solution)/shard_map/psum | solution.py:152
  205.2 3.8 copy-start.47
  205.2 6.2 copy-start.50
  205.2 32.5 %copy-start.38 = (bf16[48,768]{1,0:T(8,128)(2,1)S(1)}, bf16[48,768]{1,0:T(8,128)(2,1)}, u32[]{:S(2)}) copy-start(bf16[48,768]{1,0:T(8,128)(2,1)} %param.25) | copy-start | bytes 221188
  205.3 66.1 %copy-start.39 = (bf16[768,48]{0,1:T(8,128)(2,1)S(1)}, bf16[768,48]{0,1:T(8,128)(2,1)}, u32[]{:S(2)}) copy-start(bf16[768,48]{0,1:T(8,128)(2,1)} %param.27) | copy-start | bytes 221188
  208.9 138.8 %all-reduce.19.cloned.1.call-start = ((), (), s32[]{:S(2)}) async-start(), calls=%async_computation.10 | async-start | bytes 6291456 | tf_op jit(solution)/shard_map/psum | solution.py:206
  311.5 6.0 copy-start.1
  313.0 4.5 copy-start.21
  313.0 4.5 copy-start.28
  328.0 134.5 %reduce-scatter.12.cloned.1.call-start = ((), (), s32[]{:S(2)}) async-start(), calls=%async_computation.11 | async-start | bytes 4718592 | tf_op jit(solution)/shard_map/reduce_scatter | solution.py:236
  347.7 4.1 copy-start.2
  347.7 4.7 copy-start.5
  417.9 90.2 %reduce-scatter.14.cloned.1.call-start = ((), (), s32[]{:S(2)}) async-start(), calls=%async_computation.12 | async-start | bytes 4718592 | tf_op jit(solution)/shard_map/reduce_scatter | solution.py:237
  418.4 120.1 %all-reduce.21.cloned.1.call-start = ((), (), s32[]{:S(2)}) async-start(), calls=%async_computation.20 | async-start | bytes 6291456 | tf_op jit(solution)/shard_map/psum | solution.py:171
  515.1 117.9 %all-reduce.23.cloned.1.call-start = ((), (), s32[]{:S(2)}) async-start(), calls=%async_computation.21 | async-start | bytes 5701632 | tf_op jit(solution)/shard_map/psum | solution.py:300
  515.8 4.8 copy-start.3
  515.8 4.8 copy-start.52
  520.6 4.2 copy-start.16
  520.6 4.2 copy-start.23
  520.6 4.2 copy-start.25
  520.6 4.2 copy-start.31
  520.6 4.2 copy-start.33
  520.6 4.2 copy-start.36
  520.6 4.2 copy-start.43
  538.5 3.0 copy-start.4
  538.5 3.0 copy-start.20
  541.6 4.5 copy-start.7
  541.6 4.5 copy-start.8
  541.6 5.1 copy-start.15
  551.6 146.1 %reduce-scatter.26.cloned.1.call-start = ((), (), s32[]{:S(2)}) async-start(), calls=%async_computation.19 | async-start | bytes 221184
  558.0 204.2 %reduce-scatter.20.cloned.1.call-start = ((), (), s32[]{:S(2)}) async-start(), calls=%async_computation.15 | async-start | bytes 442368 | tf_op jit(solution)/shard_map/reduce_scatter | solution.py:316
  633.0 4.2 copy-start.27
  634.7 3.6 copy-start.26
  634.8 194.8 %reduce-scatter.18.cloned.1.call-start = ((), (), s32[]{:S(2)}) async-start(), calls=%async_computation.14 | async-start | bytes 1327104 | tf_op jit(solution)/shard_map/reduce_scatter | solution.py:314
  637.1 259.7 %reduce-scatter.22.cloned.1.call-start = ((), (), s32[]{:S(2)}) async-start(), calls=%async_computation.16 | async-start | bytes 1327104 | tf_op jit(solution)/shard_map/reduce_scatter | solution.py:318
  638.3 325.9 %reduce-scatter.24.cloned.1.call-start = ((), (), s32[]{:S(2)}) async-start(), calls=%async_computation.17 | async-start | bytes 1327104 | tf_op jit(solution)/shard_map/reduce_scatter | solution.py:320
  639.4 42.2 %copy-start.11 = (bf16[384,3,384]{2,0,1:T(8,128)(2,1)S(1)}, bf16[384,3,384]{2,0,1:T(8,128)(2,1)}, u32[]{:S(2)}) copy-start(bf16[384,3,384]{2,0,1:T(8,128)(2,1)} %copy-done.10) | copy-start | bytes 2654212
  639.4 394.8 %reduce-scatter.16.cloned.1.call-start = ((), (), s32[]{:S(2)}) async-start(), calls=%async_computation.13 | async-start | bytes 1990656 | tf_op jit(solution)/shard_map/reduce_scatter | solution.py:312
  (22 other events, 43.9 us)
Sparse Core Ops, SparseCore 0:
  121.6 25.7 all-gather.5
  148.9 27.1 all-gather.7
  209.0 23.1 all-reduce.16
  328.1 19.5 all-reduce.18
  418.0 44.5 reduce-scatter.11
  464.7 43.3 reduce-scatter.13
  515.2 23.2 all-reduce.20
  551.7 81.2 all-reduce.22
  636.6 61.0 reduce-scatter.25
  701.7 60.4 reduce-scatter.19
  766.5 62.9 reduce-scatter.17
  833.7 62.9 reduce-scatter.21
  901.1 62.9 reduce-scatter.23
  968.4 65.8 reduce-scatter.15
where the time goes:
time: 1050 us; the launch traced here: 1040 us
  waiting for transfers between devices  547 us (52%)
  blocking collectives  273 us (26%)
  matrix products  118 us (11%)
  other arithmetic  58.7 us (6%)
  local copies, waits for them, and re-layouts  25.1 us (2%)
  between operations  18.2 us (2%)
    psum x1, waiting for transfers between devices, shards(): lax.psum(full_grads[0].astype(jnp.bfloat16), 'ctx').astype(jnp.float32)  74.9 us
    reduce_scatter x1, waiting for transfers between devices, shards(): lax.psum_scatter(summed[0], 'fsdp', scatter_dimension=0, tiled=True)  70.1 us
    reduce_scatter x1, waiting for transfers between devices, shards(): lax.psum_scatter(summed[8], 'fsdp', scatter_dimension=1, tiled=True)  67.3 us
    reduce_scatter x1, waiting for transfers between devices, shards(): lax.psum_scatter(summed[2], 'fsdp', scatter_dimension=0, tiled=True)  67.3 us
    reduce_scatter x1, waiting for transfers between devices, shards(): lax.psum_scatter(summed[6], 'fsdp', scatter_dimension=0, tiled=True)  67.2 us
    reduce_scatter x1, waiting for transfers between devices, shards(): lax.psum_scatter(summed[4], 'fsdp', scatter_dimension=1, tiled=True)  63.2 us
    unnamed x2, blocking collectives  59.1 us
    reduce_scatter x1, waiting for transfers between devices, shards(): lax.psum_scatter(value_grad, 'ctx', scatter_dimension=1, tiled=True)  43.1 us
  transfers between devices with their start and end apart: 14, of which 12 were waited for; matrix products, arithmetic and copies ran while one was open for 5% of the time, Pallas kernels for 0%

commit v1 on v0

v1 whole, which is shorter than its diff:
```python
import functools
import math

import jax
import jax.numpy as jnp
from jax import lax
from jax.experimental import pallas as pl
from jax.experimental.pallas import tpu as pltpu
from jax.sharding import PartitionSpec as P

HD = 64
EPSILON = 1e-06
MESH = pl.DeviceIdType.MESH


def normalize(values):
    centre = values - jnp.mean(values, axis=-1, keepdims=True)
    inverse = lax.rsqrt(jnp.mean(centre * centre, axis=-1, keepdims=True) + EPSILON)
    return (centre * inverse, inverse)


def norm_back(upstream, normed, inverse):
    return inverse * (
        upstream
        - jnp.mean(upstream, axis=-1, keepdims=True)
        - normed * jnp.mean(upstream * normed, axis=-1, keepdims=True)
    )


def remote(src, dst, send, recv, device):
    return pltpu.make_async_remote_copy(
        src_ref=src, dst_ref=dst, send_sem=send, recv_sem=recv,
        device_id=device, device_id_type=MESH,
    )


def greet(F, f, c, t):
    barrier = pltpu.get_barrier_semaphore()
    pl.semaphore_signal(barrier, inc=1, device_id={"tp": 1 - t}, device_id_type=MESH)
    pl.semaphore_signal(barrier, inc=1, device_id={"ctx": 1 - c}, device_id_type=MESH)

    def one(k, carry):
        pl.semaphore_signal(
            barrier, inc=1, device_id={"fsdp": lax.rem(f + k, F)}, device_id_type=MESH
        )
        return carry

    lax.fori_loop(1, F, one, 0)
    pl.semaphore_wait(barrier, F + 1)


def each_peer(F, f, body):
    def one(k, carry):
        body(k, lax.rem(f + k, F), lax.rem(f + F - k, F))
        return carry

    lax.fori_loop(1, F, one, 0)


def gather_kernel(
    F, C, T,
    w_ref, x_ref, ct_ref, sc_ref, bs_ref, wm_ref,
    W, X, CT, SC, BS, MO,
    MP, MR,
    w_s, w_r, wt_s, wt_r, sc_s, sc_r, bs_s, bs_r, m_s, m_r, big_s, big_r, loc,
):
    f, c, t = lax.axis_index("fsdp"), lax.axis_index("ctx"), lax.axis_index("tp")
    greet(F, f, c, t)
    other_core, other_half = {"tp": 1 - t}, {"ctx": 1 - c}

    def sc_copy(k, to, at):
        return remote(sc_ref, SC.at[at], sc_s.at[k], sc_r.at[at], {"fsdp": to})

    def bs_copy(k, to, at):
        return remote(bs_ref, BS.at[t, at], bs_s.at[k], bs_r.at[at], {"fsdp": to})

    def w_copy(k, to, at):
        return remote(w_ref, W.at[t, at], w_s.at[k], w_r.at[at], {"fsdp": to})

    def m_copy(k, to, at):
        return remote(MP.at[to], MR.at[at], m_s.at[k], m_r.at[at], {"fsdp": to})

    def core_copy(at):
        return remote(W.at[t, at], W.at[t, at], wt_s.at[at], wt_r.at[at], other_core)

    own_first = remote(w_ref, W.at[t, f], wt_s.at[f], wt_r.at[f], other_core)
    send_x = remote(x_ref.at[T * (1 - c) + t], X.at[c], big_s.at[0], big_r.at[0], other_half)
    send_ct = remote(ct_ref.at[T * (1 - c) + t], CT.at[c], big_s.at[1], big_r.at[1], other_half)
    keep_x = pltpu.make_async_copy(x_ref.at[T * c + t], X.at[c], loc.at[0])
    keep_ct = pltpu.make_async_copy(ct_ref.at[T * c + t], CT.at[c], loc.at[1])
    keep_w = pltpu.make_async_copy(w_ref, W.at[t, f], loc.at[2])

    def start_small(k, to, source):
        sc_copy(k, to, f).start()
        bs_copy(k, to, f).start()

    each_peer(F, f, start_small)
    each_peer(F, f, lambda k, to, source: w_copy(k, to, f).start())
    send_x.start()
    send_ct.start()
    own_first.start()
    keep_x.start()
    keep_ct.start()
    keep_w.start()
    SC[f] = sc_ref[...]
    BS[t, f] = bs_ref[...]
    each_peer(F, f, lambda k, to, source: sc_copy(k, to, source).wait_recv())
    rows = SC[...].reshape(F * SC.shape[1], SC.shape[2]).astype(jnp.bfloat16)
    MP[...] = jnp.dot(rows, wm_ref[...], preferred_element_type=jnp.float32).reshape(MP.shape)
    each_peer(F, f, lambda k, to, source: m_copy(k, to, f).start())
    MR[f] = MP[f]
    each_peer(F, f, lambda k, to, source: bs_copy(k, to, source).wait_recv())
    send_bs = remote(BS.at[t], BS.at[t], big_s.at[2], big_r.at[2], other_core)
    send_bs.start()
    each_peer(F, f, lambda k, to, source: m_copy(k, to, source).wait_recv())
    MO[t] = jnp.sum(MR[...], axis=0)
    send_mo = remote(MO.at[t], MO.at[t], big_s.at[3], big_r.at[3], other_core)
    send_mo.start()

    def forward(k, to, source):
        w_copy(k, to, source).wait_recv()
        core_copy(source).start()

    each_peer(F, f, forward)

    def finish(k, to, source):
        sc_copy(k, to, f).wait_send()
        bs_copy(k, to, f).wait_send()
        w_copy(k, to, f).wait_send()
        m_copy(k, to, f).wait_send()
        core_copy(source).wait()

    each_peer(F, f, finish)
    own_first.wait()
    send_x.wait()
    send_ct.wait()
    send_bs.wait()
    send_mo.wait()
    keep_x.wait()
    keep_ct.wait()
    keep_w.wait()


def gather(mesh, packed, latents, cotangent, cond_rows, biases, mod_weight):
    F, C, T = mesh.shape["fsdp"], mesh.shape["ctx"], mesh.shape["tp"]
    half, width = latents.shape[1:]
    rows, columns = cond_rows.shape[0], mod_weight.shape[1]
    anywhere = pl.BlockSpec(memory_space=pl.ANY)
    vmem = pl.BlockSpec(memory_space=pltpu.VMEM)
    dma = pltpu.SemaphoreType.DMA
    return pl.pallas_call(
        functools.partial(gather_kernel, F, C, T),
        out_shape=(
            jax.ShapeDtypeStruct((T, F) + packed.shape, packed.dtype),
            jax.ShapeDtypeStruct((C, half, width), jnp.float32),
            jax.ShapeDtypeStruct((C, half, width), jnp.float32),
            jax.ShapeDtypeStruct((F, rows, width), jnp.float32),
            jax.ShapeDtypeStruct((T, F) + biases.shape, jnp.float32),
            jax.ShapeDtypeStruct((T, rows, columns), jnp.float32),
        ),
        in_specs=[anywhere, anywhere, anywhere, vmem, vmem, vmem],
        out_specs=(anywhere, anywhere, anywhere, vmem, vmem, vmem),
        scratch_shapes=[
            pltpu.VMEM((F, rows, columns), jnp.float32),
            pltpu.VMEM((F, rows, columns), jnp.float32),
        ] + [dma((F,))] * 10 + [dma((4,)), dma((4,)), dma((3,))],
        compiler_params=pltpu.CompilerParams(
            collective_id=0, has_side_effects=True, vmem_limit_bytes=40 << 20
        ),
        name="gather",
    )(packed, latents, cotangent, cond_rows, biases, mod_weight)


def reduce_kernel(
    F, C, T,
    gp, lg, mg_ref, wm_ref,
    GO, LO, MG, CO,
    A, S1, B, S2, R, CP, CR, CX,
    a_s, a_r, b_s, b_r, r_s, r_r, mg_s, mg_r, c_s, c_r, big_s, big_r, loc,
):
    f, c, t = lax.axis_index("fsdp"), lax.axis_index("ctx"), lax.axis_index("tp")
    deep = wm_ref.shape[1]
    greet(F, f, c, t)
    other_core, other_half = {"tp": 1 - t}, {"ctx": 1 - c}

    def mg_copy(k, to, at):
        return remote(mg_ref, MG.at[c, t, at], mg_s.at[k], mg_r.at[at], {"fsdp": to})

    def a_copy(h, at):
        return remote(gp.at[1 - t, h, at], A.at[h, at], a_s.at[h, at], a_r.at[h, at], other_core)

    def b_copy(at):
        return remote(S1.at[1 - c, at], B.at[at], b_s.at[at], b_r.at[at], other_half)

    def r_copy(to, at):
        return remote(S2.at[to], R.at[at], r_s.at[to], r_r.at[at], {"fsdp": to})

    def c_copy(to, at):
        return remote(CP.at[to], CR.at[at], c_s.at[to], c_r.at[at], {"fsdp": to})

    def over_blocks(body):
        def one(k, carry):
            body(lax.rem(f + k, F))
            return carry

        lax.fori_loop(1, F + 1, one, 0)

    each_peer(F, f, lambda k, to, source: mg_copy(k, to, f).start())

    def start_a(at):
        a_copy(1 - c, at).start()
        a_copy(c, at).start()

    over_blocks(start_a)
    own = T * c + t
    keep = pltpu.make_async_copy(lg.at[c], LO.at[own], loc)
    keep.start()
    MG[c, t, f] = mg_ref[...]

    def add(one, two):
        return (one.astype(jnp.float32) + two.astype(jnp.float32)).astype(jnp.bfloat16)

    def first(at):
        for away, h in enumerate((c, 1 - c)[::-1]):
            a_copy(h, at).wait_recv()
            S1[h, at] = add(gp[t, h, at], A[h, at])
            if away == 0:
                b_copy(at).start()

    over_blocks(first)
    send_lg = remote(lg.at[1 - c], LO.at[own], big_s.at[0], big_r.at[0], other_half)
    send_lg.start()
    each_peer(F, f, lambda k, to, source: mg_copy(k, to, source).wait_recv())
    mg_core = remote(MG.at[c, t], MG.at[c, t], big_s.at[1], big_r.at[1], other_core)
    mg_core.start()

    def second(at):
        b_copy(at).wait_recv()
        S2[at] = add(S1[c, at], B[at])

    def second_peer(k, to, source):
        second(to)
        r_copy(to, f).start()

    mg_core.wait()
    mg_half = remote(MG.at[c], MG.at[c], big_s.at[2], big_r.at[2], other_half)
    mg_half.start()
    each_peer(F, f, second_peer)
    second(f)
    mg_half.wait()
    CP[...] = jnp.zeros_like(CP)
    for c2 in range(C):
        for t2 in range(T):
            total = jnp.zeros((F, deep), jnp.float32)
            for k in range(3):
                row = jnp.where(t == 0, MG[c2, t2, :, k, :], MG[c2, t2, :, 3 + k, :])
                total += lax.dot_general(
                    row, wm_ref[k].astype(jnp.float32), (((1,), (1,)), ((), ())),
                    precision=lax.Precision.HIGHEST, preferred_element_type=jnp.float32,
                )
            CP[:, T * c2 + t2, 0:deep] = total
    each_peer(F, f, lambda k, to, source: c_copy(to, f).start())
    CR[f] = CP[f]
    send_lg.wait_recv()
    keep.wait()

    def core_lg(n, at):
        return remote(LO.at[at], LO.at[at], big_s.at[3 + n], big_r.at[3 + n], other_core)

    core_lg(0, own).start()
    core_lg(1, T * (1 - c) + t).start()
    R[f] = S2[f]
    each_peer(F, f, lambda k, to, source: r_copy(to, source).wait_recv())
    total = lax.fori_loop(
        0, F, lambda k, sum_: sum_ + R[k].astype(jnp.float32),
        jnp.zeros(R.shape[1:], jnp.float32),
    )
    GO[c] = total.astype(jnp.bfloat16)
    go_half = remote(GO.at[c], GO.at[c], big_s.at[5], big_r.at[5], other_half)
    go_half.start()
    each_peer(F, f, lambda k, to, source: c_copy(to, source).wait_recv())
    c_core = remote(CR, CX, big_s.at[6], big_r.at[6], other_core)
    c_core.start()
    c_core.wait()
    CO[...] = CR[...] + CX[...]

    def finish(k, to, source):
        mg_copy(k, to, f).wait_send()
        r_copy(to, f).wait_send()
        c_copy(to, f).wait_send()

    each_peer(F, f, finish)

    def finish_block(at):
        a_copy(1 - c, at).wait_send()
        a_copy(c, at).wait_send()
        b_copy(at).wait_send()

    over_blocks(finish_block)
    send_lg.wait_send()
    go_half.wait()
    core_lg(0, own).wait()
    core_lg(1, T * (1 - c) + t).wait()


def reduce(mesh, grads, latents_grad, mod_grad, mod_weight):
    F, C, T = mesh.shape["fsdp"], mesh.shape["ctx"], mesh.shape["tp"]
    half, width = latents_grad.shape[1:]
    block = grads.shape[3:]
    anywhere = pl.BlockSpec(memory_space=pl.ANY)
    vmem = pl.BlockSpec(memory_space=pltpu.VMEM)
    dma = pltpu.SemaphoreType.DMA
    low = jnp.bfloat16
    return pl.pallas_call(
        functools.partial(reduce_kernel, F, C, T),
        out_shape=(
            jax.ShapeDtypeStruct((C,) + block, low),
            jax.ShapeDtypeStruct((C * T, half, width), jnp.float32),
            jax.ShapeDtypeStruct((C, T, F) + mod_grad.shape, jnp.float32),
            jax.ShapeDtypeStruct((F, 8, 128), jnp.float32),
        ),
        in_specs=[vmem, anywhere, vmem, vmem],
        out_specs=(vmem, anywhere, vmem, vmem),
        scratch_shapes=[
            pltpu.VMEM((C, F) + block, low),
            pltpu.VMEM((C, F) + block, low),
            pltpu.VMEM((F,) + block, low),
            pltpu.VMEM((F,) + block, low),
            pltpu.VMEM((F,) + block, low),
            pltpu.VMEM((F, 8, 128), jnp.float32),
            pltpu.VMEM((F, 8, 128), jnp.float32),
            pltpu.VMEM((F, 8, 128), jnp.float32),
            dma((C, F)), dma((C, F)),
        ] + [dma((F,))] * 8 + [dma((7,)), dma((7,)), dma],
        compiler_params=pltpu.CompilerParams(
            collective_id=1, has_side_effects=True, vmem_limit_bytes=56 << 20
        ),
        name="reduce",
    )(grads, latents_grad, mod_grad, mod_weight)


def attend_forward(blocks):
    query_rows, key_rows, value_rows = blocks
    scores = jnp.einsum(
        "qc,kc->qk", query_rows, key_rows, preferred_element_type=jnp.float32
    ) * (1.0 / math.sqrt(HD))
    highest = jnp.max(scores, axis=-1, keepdims=True)
    exponent = jnp.exp(scores - highest)
    totals = jnp.sum(exponent, axis=-1, keepdims=True)
    softmax_rows = (exponent / totals).astype(jnp.bfloat16)
    mixed_rows = jnp.dot(softmax_rows, value_rows, preferred_element_type=jnp.float32)
    return (mixed_rows.astype(jnp.bfloat16), highest + jnp.log(totals))


def attend_backward(blocks):
    query_rows, key_rows, value_rows, attended_grad, log_totals = blocks
    factor = 1.0 / math.sqrt(HD)
    scores = (
        jnp.einsum("qc,kc->qk", query_rows, key_rows, preferred_element_type=jnp.float32) * factor
    )
    softmax_rows = jnp.exp(scores - log_totals)
    prob_grad = jnp.einsum(
        "qc,kc->qk", attended_grad, value_rows, preferred_element_type=jnp.float32
    )
    row_inner = jnp.sum(prob_grad * softmax_rows, axis=-1, keepdims=True)
    score_grad = (softmax_rows * (prob_grad - row_inner)).astype(jnp.bfloat16)
    query_grad = jnp.dot(score_grad, key_rows, preferred_element_type=jnp.float32) * factor
    key_grad = (
        jnp.einsum("qk,qc->kc", score_grad, query_rows, preferred_element_type=jnp.float32) * factor
    )
    value_grad = jnp.einsum(
        "qk,qc->kc",
        softmax_rows.astype(jnp.bfloat16),
        attended_grad,
        preferred_element_type=jnp.float32,
    )
    low = jnp.bfloat16
    return (query_grad.astype(low), key_grad.astype(low), value_grad.astype(low))


def attention(queries, keys, values):
    return lax.map(attend_forward, (queries, keys, values))


def attention_back(queries, keys, values, attended_grad, log_totals):
    return lax.map(attend_backward, (queries, keys, values, attended_grad, log_totals))


def split_heads(rows):
    return rows.reshape(rows.shape[0], rows.shape[1] // HD, HD).transpose(1, 0, 2)


def join_heads(heads):
    return heads.transpose(1, 0, 2).reshape(heads.shape[1], heads.shape[0] * heads.shape[2])


def dot(a, b):
    return jnp.dot(a, b, preferred_element_type=jnp.float32)


def dot_bt(a, b):
    return lax.dot_general(a, b, (((1,), (1,)), ((), ())), preferred_element_type=jnp.float32)


def dot_at(a, b):
    return lax.dot_general(a, b, (((0,), (0,)), ((), ())), preferred_element_type=jnp.float32)


def shards(
    mesh,
    latents_in,
    condition,
    w_mod,
    b_mod,
    w_qkv,
    b_qv,
    w_out,
    b_out,
    up_weight,
    up_projection_bias,
    down_weight,
    down_projection_bias,
    cotangent,
):
    F, C, T = mesh.shape["fsdp"], mesh.shape["ctx"], mesh.shape["tp"]
    f, c, t = lax.axis_index("fsdp"), lax.axis_index("ctx"), lax.axis_index("tp")
    group, half, width = latents_in.shape
    assert C == 2 and T == 2 and group == C * T
    deep = w_mod.shape[0]
    part = w_qkv.shape[2]
    hidden = up_weight.shape[1]
    low = jnp.bfloat16
    full = jnp.float32
    own = T * c + t

    packed = jnp.concatenate(
        [w_qkv.reshape(deep, 3 * part), w_out.T, up_weight, down_weight.T], axis=1
    )
    columns = packed.shape[1]
    flat_bias = jnp.concatenate(
        [
            b_mod.reshape(-1), b_qv.reshape(-1), b_out, up_projection_bias, down_projection_bias,
        ]
    ).astype(full)
    bias_rows = -(-flat_bias.shape[0] // 1024) * 8
    biases = jnp.pad(flat_bias, (0, bias_rows * 128 - flat_bias.shape[0])).reshape(bias_rows, 128)
    silu_cond = jax.nn.silu(condition).astype(low)
    cond_rows = jnp.pad(silu_cond.astype(full), ((0, 8 - group), (0, 0)))
    mod_padded = lax.dynamic_update_slice(
        jnp.zeros((width, 3 * width), low), w_mod.reshape(deep, 3 * width), (f * deep, 0)
    )
    weights, x, cot, cond_all, bias_all, mod_all = gather(
        mesh, packed, latents_in, cotangent, cond_rows, biases, mod_padded
    )
    x = x.reshape(C * half, width)
    cot = cot.reshape(C * half, width)
    weights = weights.reshape(T, width, columns)

    def cut(tensor, start, size):
        return tensor[:, :, start : start + size]

    qkv_full = (
        cut(weights, 0, 3 * part).reshape(T, width, 3, part).transpose(1, 2, 0, 3)
        .reshape(width, 3 * width)
    )
    outs_t = cut(weights, 3 * part, part).transpose(1, 0, 2).reshape(width, width)
    up_full = cut(weights, 4 * part, hidden).transpose(1, 0, 2).reshape(width, T * hidden)
    down_t = cut(weights, 4 * part + hidden, hidden).transpose(1, 0, 2).reshape(width, T * hidden)

    bias_all = bias_all.reshape(T, F, -1)
    edges = [3 * deep, b_qv.size, b_out.size, up_projection_bias.size, down_projection_bias.size]
    pieces, start = [], 0
    for size in edges:
        pieces.append(bias_all[:, :, start : start + size])
        start += size
    mod_bias = pieces[0].reshape(T, F, 3, deep).transpose(0, 2, 1, 3).reshape(6, width)
    qv_bias = pieces[1].reshape(T, F, 2, -1).transpose(2, 0, 1, 3).reshape(2, width)
    out_bias = pieces[2][0].reshape(width)
    up_bias = pieces[3].reshape(T * hidden)
    down_bias = pieces[4][0].reshape(width)

    modulation = lax.dynamic_index_in_dim(mod_all, own, 1, keepdims=False)
    modulation = modulation.reshape(6, width) + mod_bias
    shift_one, scale_one, gate_one, shift_two, scale_two, gate_two = (
        modulation[k : k + 1] for k in range(6)
    )

    normed_one, inverse_one = normalize(x)
    hidden_one = (normed_one * (1.0 + scale_one) + shift_one).astype(low)
    projected = dot(hidden_one, qkv_full)
    queries = split_heads((projected[:, :width] + qv_bias[0]).astype(low))
    keys = split_heads(projected[:, width : 2 * width].astype(low))
    values = split_heads((projected[:, 2 * width :] + qv_bias[1]).astype(low))
    attended_heads, log_totals = attention(queries, keys, values)
    attended = join_heads(attended_heads)
    branch = dot_bt(attended, outs_t) + out_bias
    middle = x + gate_one * branch
    normed_two, inverse_two = normalize(middle)
    hidden_two = (normed_two * (1.0 + scale_two) + shift_two).astype(low)
    upper_in = dot(hidden_two, up_full) + up_bias
    gelu_value, gelu_pull = jax.vjp(lambda u: jax.nn.gelu(u, approximate=True), upper_in)
    active = gelu_value.astype(low)
    mlp_out = dot_bt(active, down_t) + down_bias
    block_own = (middle + gate_two * mlp_out).reshape(C, half, width)

    away = lax.dynamic_index_in_dim(block_own, 1 - c, 0, keepdims=False)
    here = lax.dynamic_index_in_dim(block_own, c, 0, keepdims=False)
    landed = lax.ppermute(away, "ctx", [(0, 1), (1, 0)])
    pair = jnp.where(c == 0, jnp.stack([here, landed]), jnp.stack([landed, here]))
    other_pair = lax.ppermute(pair, "tp", [(0, 1), (1, 0)])
    block_out = jnp.where(
        t == 0, jnp.stack([pair, other_pair], 1), jnp.stack([other_pair, pair], 1)
    ).reshape(group, half, width)

    gate_two_grad = jnp.sum(cot * mlp_out, axis=0)
    down_in = (cot * gate_two).astype(low)
    down_bias_grad = jnp.sum(down_in, axis=0, dtype=full)
    down_grad_t = dot_at(down_in, active)
    upper_grad = gelu_pull(dot(down_in, down_t))[0].astype(low)
    up_bias_grad = jnp.sum(upper_grad, axis=0, dtype=full)
    up_grad = dot_at(hidden_two, upper_grad)
    hidden_two_grad = dot_bt(upper_grad, up_full)
    scale_two_grad = jnp.sum(hidden_two_grad * normed_two, axis=0)
    shift_two_grad = jnp.sum(hidden_two_grad, axis=0)
    middle_grad = cot + norm_back(hidden_two_grad * (1.0 + scale_two), normed_two, inverse_two)
    gate_one_grad = jnp.sum(middle_grad * branch, axis=0)
    branch_grad = (middle_grad * gate_one).astype(low)
    out_bias_grad = jnp.sum(branch_grad, axis=0, dtype=full)
    out_grad_t = dot_at(branch_grad, attended)
    attended_grad = split_heads(dot(branch_grad, outs_t).astype(low))
    query_grad, key_grad, value_grad = attention_back(
        queries, keys, values, attended_grad, log_totals
    )
    projected_grad = jnp.concatenate(
        [join_heads(query_grad), join_heads(key_grad), join_heads(value_grad)], axis=1
    )
    all_bias_grad = jnp.sum(projected_grad, axis=0, dtype=full)
    qkv_grad = dot_at(hidden_one, projected_grad)
    hidden_one_grad = dot_bt(projected_grad, qkv_full)
    scale_one_grad = jnp.sum(hidden_one_grad * normed_one, axis=0)
    shift_one_grad = jnp.sum(hidden_one_grad, axis=0)
    latents_grad = middle_grad + norm_back(
        hidden_one_grad * (1.0 + scale_one), normed_one, inverse_one
    )
    zeros = jnp.zeros((width,), full)
    mod_grad = jnp.stack(
        [
            shift_one_grad, scale_one_grad, gate_one_grad,
            shift_two_grad, scale_two_grad, gate_two_grad, zeros, zeros,
        ]
    )

    def by_owner(grad, size):
        return grad.astype(low).reshape(F, deep, T, size).transpose(2, 0, 1, 3)

    grads = jnp.concatenate(
        [
            qkv_grad.astype(low).reshape(F, deep, 3, T, part).transpose(3, 0, 1, 2, 4)
            .reshape(T, F, deep, 3 * part),
            by_owner(out_grad_t, part),
            by_owner(up_grad, hidden),
            by_owner(down_grad_t, hidden),
        ],
        axis=3,
    )
    grads = grads.reshape(T, F, deep, C, columns // C).transpose(0, 3, 1, 2, 4)
    bias_grads = jnp.concatenate(
        [
            all_bias_grad.reshape(3, T, F, -1)[0::2].transpose(1, 2, 0, 3).reshape(T, F, -1),
            up_bias_grad.reshape(T, F, -1),
            jnp.broadcast_to(out_bias_grad.reshape(1, F, deep), (T, F, deep)),
            jnp.broadcast_to(down_bias_grad.reshape(1, F, deep), (T, F, deep)),
        ],
        axis=2,
    ).astype(low)
    extra = bias_grads.shape[2] // deep
    bias_grads = jnp.pad(
        bias_grads.reshape(T, 1, F, deep, extra),
        ((0, 0), (0, C - 1), (0, 0), (0, 0), (0, 128 - extra)),
    )
    grads = jnp.concatenate([grads, bias_grads], axis=4)
    owned, latents_grad, mod_grads, cond_parts = reduce(
        mesh, grads, latents_grad.reshape(C, half, width), mod_grad, w_mod.transpose(1, 0, 2)
    )
    owned = owned.astype(full)
    wide = owned[:, :, : columns // C].transpose(1, 0, 2).reshape(deep, columns)
    own_bias = owned[0, :, columns // C : columns // C + extra].reshape(-1)
    qv_size, up_size = b_qv.size, up_projection_bias.size
    qkv_owned = wide[:, : 3 * part].reshape(deep, 3, part)
    out_owned = wide[:, 3 * part : 4 * part].T
    up_owned = wide[:, 4 * part : 4 * part + hidden]
    down_owned = wide[:, 4 * part + hidden :].T

    all_mod = mod_grads.transpose(2, 0, 1, 3, 4).reshape(F * group, 8, width)
    own_mod = lax.dynamic_slice_in_dim(all_mod, t * 3, 3, axis=1)
    cond_own = lax.dynamic_slice_in_dim(cond_all[:, :group], f * deep, deep, axis=2)
    mod_weight_grad = jnp.einsum(
        "ld,lkc->dkc", cond_own.reshape(F * group, deep), own_mod,
        precision=lax.Precision.HIGHEST,
    )
    mod_bias_grad = lax.dynamic_slice_in_dim(jnp.sum(own_mod, axis=0), f * deep, deep, axis=1)
    silu_total = cond_parts[:, :group, :deep].transpose(1, 0, 2).reshape(group, width)
    condition_grad = jax.vjp(jax.nn.silu, condition)[1](silu_total)[0]
    return (
        block_out,
        latents_grad,
        condition_grad,
        mod_weight_grad,
        mod_bias_grad,
        qkv_owned,
        own_bias[:qv_size].reshape(2, -1),
        out_owned,
        own_bias[qv_size + up_size : qv_size + up_size + deep],
        up_owned,
        own_bias[qv_size : qv_size + up_size],
        down_owned,
        own_bias[qv_size + up_size + deep : qv_size + up_size + 2 * deep],
    )


def solution(mesh):
    placed = (
        P("fsdp", "ctx", None),
        P("fsdp", None),
        P("fsdp", "tp", None),
        P("tp", "fsdp"),
        P("fsdp", None, "tp"),
        P(None, ("tp", "fsdp")),
        P("tp", "fsdp"),
        P("fsdp"),
        P("fsdp", "tp"),
        P(("tp", "fsdp")),
        P("tp", "fsdp"),
        P("fsdp"),
        P("fsdp", "ctx", None),
    )
    return jax.shard_map(
        functools.partial(shards, mesh),
        mesh=mesh,
        in_specs=placed,
        out_specs=(
            P("fsdp", "ctx", None),
            P("fsdp", "ctx", None),
            P("fsdp", None),
            P("fsdp", "tp", None),
            P("tp", "fsdp"),
            P("fsdp", None, "tp"),
            P(None, ("tp", "fsdp")),
            P("tp", "fsdp"),
            P("fsdp"),
            P("fsdp", "tp"),
            P(("tp", "fsdp")),
            P("tp", "fsdp"),
            P("fsdp"),
        ),
        check_vma=False,
    )
```

time: 1050 us -> 403 us (0.38)
  waiting for transfers between devices: 547 us -> 0.01 us
  blocking collectives: 273 us -> 0 us
  Pallas kernels: 0 us -> 117 us
  local copies, waits for them, and re-layouts: 25.1 us -> 105 us
  other arithmetic: 58.7 us -> 33.7 us
  between operations: 18.2 us -> 1.53 us
  matrix products: 118 us -> 129 us
    reduce_scatter x7 -> x0, waiting for transfers between devices: 417 us -> none  [the longest x1 70.1 us: shards(): lax.psum_scatter(summed[0], 'fsdp', scatter_dimension=0, tiled=True)]
    all_gather x8 -> x0, blocking collectives: 203 us -> none  [the longest x1 33.7 us: shards(): lax.all_gather(down_weight, 'fsdp', axis=1, tiled=True)]
    pallas_call x0 -> x2, Pallas kernels: none -> 117 us  [the longest x1 60.5 us: reduce(): pl.pallas_call(functools.partial(reduce_kernel, F, C, T), out_shape=(jax....]
    psum x4 -> x0, waiting for transfers between devices: 105 us -> none  [the longest x1 74.9 us: shards(): lax.psum(full_grads[0].astype(jnp.bfloat16), 'ctx').astype(jnp.float32)]
    unnamed x2 -> x0, blocking collectives: 59.1 us -> none
    reduce_sum x9 -> x4, other arithmetic: 24.1 us -> 3.15 us  [the longest x1 1.99 us: shards(): all_bias_grad = jnp.sum(projected_grad, axis=0, dtype=full)]
    reshape x0 -> x26, local copies, waits for them, and re-layouts: none -> 19.9 us  [the longest x6 8.72 us: by_owner(): return grad.astype(low).reshape(F, deep, T, size).transpose(2, 0, 1, 3)]
    all_gather x2 -> x0, waiting for transfers between devices: 16.1 us -> none  [the longest x1 16.1 us: shards(): lax.all_gather(key_rows, 'ctx', axis=1, tiled=True)]
  transfers between devices with their start and end apart: 14 -> 2, of which waited for: 12 -> 0; matrix products, arithmetic and copies ran while one was open for 5% -> 33% of each run, Pallas kernels for 0% -> 15%
where the time goes in v1:
time: 403 us; the launch traced here: 397 us
  matrix products  129 us (32%)
  Pallas kernels  117 us (29%)
  local copies, waits for them, and re-layouts  105 us (26%)
  other arithmetic  33.7 us (8%)
  loops' own time  9.68 us (2%)
    pallas_call x1, Pallas kernels, reduce(): pl.pallas_call(functools.partial(reduce_kernel, F, C, T), out_shape=(jax....  60.5 us
    pallas_call x1, Pallas kernels, gather(): pl.pallas_call(functools.partial(gather_kernel, F, C, T), out_shape=(jax....  56.7 us
    unnamed x102, local copies, waits for them, and re-layouts  24.1 us
    dot_general x4, matrix products, dot_bt(): lax.dot_general(a, b, (((1,), (1,)), ((), ())), preferred_element_type=jn...  18.4 us
    dot_general x6, matrix products, attend_forward(): jnp.dot(softmax_rows, value_rows, preferred_element_type=jnp.float32)  15.6 us
    dot_general x4, matrix products, dot(): return jnp.dot(a, b, preferred_element_type=jnp.float32)  14.5 us
    dot_general x6, matrix products, attend_backward(): jnp.einsum('qk,qc->kc', score_grad, query_rows, preferred_element_type=jn...  14.3 us
    dot_general x6, matrix products, attend_backward(): jnp.dot(score_grad, key_rows, preferred_element_type=jnp.float32) * factor  12.8 us
  transfers between devices with their start and end apart: 2, of which 0 were waited for; matrix products, arithmetic and copies ran while one was open for 33% of the time, Pallas kernels for 15%

profile of v1, /device:TPU:0, one launch (start us, length us, event | category | flops | bytes accessed | tf_op | source)
XLA Modules:
  0.0 396.5 jit_solution(7223955120783868086)
XLA Ops:
  13.1 56.7 %gather.1 = (bf16[2,8,48,2304]{3,2,1,0:T(8,128)(2,1)S(1)}, f32[2,512,384]{2,1,0:T(8,128)S(1)}, f32[2,512,384]{2,1,0:T(8,128)S(1)}, f32[8,8,384]{2,1,0:T(8,128)S(...) custom-call(bf16[48,2304]{1,0:T(8,128)(2,1)S(1)} %concatenate.33.w_ref, f32[4,512,384]{2,1,0:T(8,128)S(1)} %copy-done.3, ...), custom_call_target="tpu_custom_call" | custom-call | tf_op jit(solution)/shard_map/gather/pallas_call | solution.py:151
  74.4 2.2 slice.148
  76.7 3.2 fusion.84
  88.1 2.2 copy.94
  90.2 2.2 copy.67
  92.4 2.4 copy.97
  94.8 2.4 copy.96
  102.2 2.3 copy.70
  104.5 2.3 copy.69
  106.8 2.5 copy.72
  109.3 2.5 copy.73
  111.7 2.3 copy.68
  114.0 2.4 copy.71
  117.5 34.1 %while.26 = (s32[]{:T(128)}, bf16[6,1024,64]{1,2,0:T(8,128)(2,1)}, f32[6,1024,1]{1,2,0:T(1,128)}, bf16[6,1024,64]{2,1,0:T(8,128)(2,1)}, bf16[6,1024,64]{2,1,0:T(...) while((s32[]{:T(128)}, bf16[6,1024,64]{1,2,0:T(8,128)(2,1)}, f32[6,1024,1]{1,2,0:T(1,128)}, ...), condition=%wide.region_5.6_spmd, body=%wide.region_2.5_spmd.sunk | while | flops 277937152 | bytes 13543513 | solution.py:382
  119.9 2.6 fusion.129
  125.6 2.6 fusion.129
  131.3 2.6 fusion.129
  137.0 2.6 fusion.129
  142.7 2.6 fusion.129
  148.4 2.6 fusion.129
  151.6 3.1 fusion.83
  156.5 4.7 %multiply_convert_fusion.1 = (bf16[1024,1536]{1,0:T(8,128)(2,1)}, f32[1024,1536]{1,0:T(8,128)S(1)}) fusion(f32[1536]{0:T(1024)S(1)} %copy-done.41, bf16[384,1536]{0,1:T(8,128)(2,1)S(1)} %bitcast.283, f32[1024,384]{1,0:T(8,128)S(1)} %get-tuple-element.231, f32[384]{0:T(512)S(1)} %get-tuple-element.187, f32[384]{0:T(512)S(1)} %get-tuple-element.188, ...), kind=kOutput, calls=%fused_computation.70 | convolution fusion | flops 1225654272 | bytes 12207104 | tf_op jit(solution)/shard_map/dot_general | solution.py:398
  161.2 6.8 %fusion.87 = (bf16[1536]{0:T(1024)(128)(2,1)}, bf16[1024,1536]{1,0:T(8,128)(2,1)S(1)}) fusion(f32[1024,1536]{1,0:T(8,128)S(1)} %get-tuple-element.261, f32[1536]{0:T(1024)S(1)} %copy-done.41, bf16[1024,384]{1,0:T(8,128)(2,1)S(1)} %bitcast.286, bf16[384,1536]{0,1:T(8,128)(2,1)S(1)} %bitcast.254), kind=kOutput, calls=%fused_computation.169 | convolution fusion | flops 1242561024 | bytes 11412480 | tf_op jit(solution)/shard_map/dot_general | solution.py:398
  169.7 3.7 multiply_reduce_fusion.2
  174.1 7.6 %fusion.67 = (f32[384]{0:T(512)}, f32[1024,384]{1,0:T(8,128)S(1)}, f32[384]{0:T(512)}, f32[1024,384]{1,0:T(8,128)}, bf16[1024,384]{1,0:T(8,128)(2,1)}) fusion(f32[2,512,384]{2,1,0:T(8,128)S(1)} %get-tuple-element.111, f32[384]{0:T(512)} %add.209, f32[1024,384]{1,0:T(8,128)} %copy-done.6, f32[384]{0:T(512)} %get-tuple-element.186, ...), kind=kOutput, calls=%fused_computation.89 | convolution fusion | flops 1214643456 | bytes 14573056 | tf_op jit(solution)/shard_map/dot_general | solution.py:402
  184.0 4.6 %convolution_convert_fusion.2 = bf16[384,1536]{1,0:T(8,128)(2,1)} fusion(bf16[1024,1536]{1,0:T(8,128)(2,1)} %copy-done.16, f32[1024,384]{1,0:T(8,128)S(1)} %copy-done.7, f32[384]{0:T(512)S(1)} %get-tuple-element.187, f32[384]{0:T(512)S(1)} %get-tuple-element.188, f32[1024]{0:T(1024)S(1)} %add_rsqrt_fusion, f32[1024]{0:T(1024)S(1)} %broadcast_multiply_fusion.4), kind=kOutput, calls=%fused_computation.76 | convolution fusion | flops 1210515456 | bytes 5909504 | tf_op jit(solution)/shard_map/dot_general | solution.py:406
  193.2 2.5 copy.116
  195.7 4.3 %convolution_convert_fusion.1 = bf16[384,1536]{1,0:T(8,128)(2,1)} fusion(bf16[1024,384]{1,0:T(8,128)(2,1)S(1)} %copy-done.23, bf16[1024,1536]{1,0:T(8,128)(2,1)} %get-tuple-element.260), kind=kOutput, calls=%fused_computation.75 | convolution fusion | flops 1208549376 | bytes 5111808 | tf_op jit(solution)/shard_map/dot_general | solution.py:406
  200.0 2.9 reshape.395
  210.1 78.9 %while.27 = (s32[]{:T(128)}, bf16[6,1024,64]{1,2,0:T(8,128)(2,1)}, bf16[6,1024,64]{1,2,0:T(8,128)(2,1)}, bf16[6,1024,64]{1,2,0:T(8,128)(2,1)}, bf16[6,1024,64]{2...) while((s32[]{:T(128)}, bf16[6,1024,64]{1,2,0:T(8,128)(2,1)}, ...), condition=%wide.region_12.13_spmd, body=%wide.region_10.12_spmd.sunk | while | flops 683998208 | bytes 33719408 | solution.py:386
  226.6 2.4 fusion.140
  229.0 2.1 fusion.139
  238.2 2.4 fusion.140
  240.5 2.1 fusion.139
  249.7 2.4 fusion.140
  261.3 2.4 fusion.140
  263.6 2.1 fusion.139
  272.8 2.4 fusion.140
  275.2 2.1 fusion.139
  284.4 2.4 fusion.140
  286.8 2.1 fusion.139
  291.5 4.0 %multiply_reduce_fusion.4 = (f32[384]{0:T(512)S(1)}, f32[1024]{0:T(1024)S(1)}, f32[1024]{0:T(1024)S(1)}, f32[384]{0:T(512)S(1)}, f32[1024,384]{1,0:T(8,128)S(1)}) fusion(f32[2,512,384]{2,1,0:T(8,128)S(1)} %get-tuple-element.105, f32[1024]{0:T(1024)S(1)} %bitcast.300, f32[1024]{0:T(1024)S(1)} %bitcast.298, f32[384]{0:T(512)S(1)} %copy-done.31, ...), kind=kOutput, calls=%fused_computation.96 | convolution fusion | flops 916583680 | bytes 6410752 | tf_op jit(solution)/shard_map/dot_general | solution.py:402
  300.4 2.3 reshape.392
  302.7 6.3 %concatenate.36 = bf16[2,8,48,2304]{3,2,1,0:T(8,128)(2,1)} concatenate(bf16[2,8,48,576]{3,2,1,0:T(8,128)(2,1)} %reshape.392, bf16[2,8,48,192]{3,2,1,0:T(8,128)(2,1)S(1)} %bitcast.282, bf16[2,8,48,768]{3,2,1,0:T(8,128)(2,1)S(1)} %bitcast.251, bf16[2,8,48,768]{3,2,1,0:T(8,128)(2,1)} %bitcast.252), dimensions={3} | concatenate | bytes 7077888 | tf_op jit(solution)/shard_map/concatenate | solution.py:556
  309.0 2.3 copy.113
  314.1 60.5 %reduce.34 = (bf16[2,48,1280]{2,1,0:T(8,128)(2,1)}, f32[4,512,384]{2,1,0:T(8,128)}, f32[2,2,8,8,384]{4,3,2,1,0:T(8,128)}, f32[8,8,128]{2,1,0:T(8,128)}) custom-call(bf16[2,2,8,48,1280]{4,3,2,1,0:T(8,128)(2,1)} %fusion.63.gp, f32[2,512,384]{2,1,0:T(8,128)} %bitcast.248, f32[8,384]{1,0:T(8,128)} %stack.73.mg_ref, bf16[3,48,384]{2,1,0:T(8,128)(2,1)} %bitcast.290), custom_call_target="tpu_custom_call" | custom-call | tf_op jit(solution)/shard_map/reduce/pallas_call | solution.py:314
  377.5 2.8 maximum_select_fusion.2
  389.5 2.2 maximum_select_fusion
  (268 shorter events, 138.8 us)
Async XLA Ops:
  0.6 7.4 %copy-start.26 = (bf16[768,48]{0,1:T(8,128)(2,1)S(1)}, bf16[768,48]{0,1:T(8,128)(2,1)}, u32[]{:S(2)}) copy-start(bf16[768,48]{0,1:T(8,128)(2,1)} %param.27) | copy-start | bytes 221188
  0.7 7.4 %copy-start.25 = (bf16[48,768]{1,0:T(8,128)(2,1)S(1)}, bf16[48,768]{1,0:T(8,128)(2,1)}, u32[]{:S(2)}) copy-start(bf16[48,768]{1,0:T(8,128)(2,1)} %param.25) | copy-start | bytes 221188
  0.7 7.4 %copy-start.27 = (bf16[192,48]{0,1:T(8,128)(2,1)S(1)}, bf16[192,48]{0,1:T(8,128)(2,1)}, u32[]{:S(2)}) copy-start(bf16[192,48]{0,1:T(8,128)(2,1)} %param.23) | copy-start | bytes 55300
  7.1 0.9 copy-start.1
  8.1 1.2 copy-start.2
  9.3 1.9 copy-start.3
  11.2 1.9 copy-start.4
  69.8 1.8 copy-start
  72.2 7.7 %copy-start.24 = (f32[2,8,1024]{2,1,0:T(8,128)}, f32[2,8,1024]{2,1,0:T(8,128)S(1)}, u32[]{:S(2)}) copy-start(f32[2,8,1024]{2,1,0:T(8,128)S(1)} %reshape.371) | copy-start | bytes 196612
  80.8 5.3 %slice-start = ((f32[2,8,1024]{2,1,0:T(8,128)}), f32[2,8,144]{2,1,0:T(8,128)S(1)}, s32[]{:S(2)}) async-start(f32[2,8,1024]{2,1,0:T(8,128)} %copy-done.24), calls=%async_computation | async-start | bytes 32768 | tf_op jit(solution)/shard_map/slice | solution.py:474
  86.8 10.3 %copy-start.29 = (f32[384]{0:T(512)}, f32[384]{0:T(512)S(1)}, u32[]{:S(2)}) copy-start(f32[384]{0:T(512)S(1)} %get-tuple-element.189) | copy-start | bytes 4612
  97.2 1.2 copy-start.14
  99.8 1.0 copy-start.37
  99.8 1.0 copy-start.38
  117.4 34.1 %copy-start.32 = (f32[384]{0:T(512)S(1)}, f32[384]{0:T(512)}, u32[]{:S(2)}) copy-start(f32[384]{0:T(512)} %get-tuple-element.191) | copy-start | bytes 4612
  154.7 13.3 %copy-start.6 = (f32[1024,384]{1,0:T(8,128)}, f32[1024,384]{1,0:T(8,128)S(1)}, u32[]{:S(2)}) copy-start(f32[1024,384]{1,0:T(8,128)S(1)} %get-tuple-element.231) | copy-start | bytes 4718596
  154.7 0.7 copy-start.34
  155.1 1.4 copy-start.22
  155.1 1.4 copy-start.41
  156.5 4.7 %copy-start.13 = (bf16[2,384,768]{1,2,0:T(8,128)(2,1)S(1)}, bf16[2,384,768]{1,2,0:T(8,128)(2,1)}, u32[]{:S(2)}) copy-start(bf16[2,384,768]{1,2,0:T(8,128)(2,1)} %copy.97) | copy-start | bytes 3538948
  168.0 1.7 copy-start.16
  181.7 2.3 copy-start.7
  183.0 194.5 %collective-permute-start = (f32[512,384]{1,0:T(8,128)}, f32[512,384]{1,0:T(8,128)}, u32[]{:S(2)}, u32[]{:S(2)}) collective-permute-start(f32[512,384]{1,0:T(8,128)} %get-tuple-element.248), channel_id=1, source_target_pairs={{0,2},{2,0},{1,3},{3,1},{4,6},{6,4},{5,7},{7,5},{8,10},{10,8},{9,1... | collective-permute-start | bytes 2359304 | tf_op jit(solution)/shard_map/ppermute | solution.py:508
  184.0 4.6 %copy-start.8 = (f32[1024,384]{1,0:T(8,128)S(1)}, f32[1024,384]{1,0:T(8,128)}, u32[]{:S(2)}) copy-start(f32[1024,384]{1,0:T(8,128)} %get-tuple-element.245) | copy-start | bytes 4718596
  184.0 4.6 %copy-start.33 = (f32[384]{0:T(512)S(1)}, f32[384]{0:T(512)}, u32[]{:S(2)}) copy-start(f32[384]{0:T(512)} %get-tuple-element.191) | copy-start | bytes 4612
  188.6 1.1 copy-start.20
  189.7 2.2 copy-start.35
  189.7 2.2 copy-start.36
  189.7 2.2 copy-start.42
  189.7 2.3 copy-start.43
  189.7 2.4 copy-start.12
  193.2 2.5 copy-start.23
  288.9 2.5 copy-start.31
  291.5 4.1 %copy-start.9 = (f32[1024,384]{1,0:T(8,128)S(1)}, f32[1024,384]{1,0:T(8,128)}, u32[]{:S(2)}) copy-start(f32[1024,384]{1,0:T(8,128)} %get-tuple-element.245) | copy-start | bytes 4718596
  291.5 4.1 %copy-start.30 = (f32[384]{0:T(512)S(1)}, f32[384]{0:T(512)}, u32[]{:S(2)}) copy-start(f32[384]{0:T(512)} %copy-done.29) | copy-start | bytes 4612
  295.5 2.1 copy-start.17
  295.5 2.1 copy-start.18
  295.5 2.0 copy-start.19
  300.4 2.3 copy-start.11
  300.4 2.3 copy-start.21
  311.3 2.1 copy-start.45
  311.3 2.1 copy-start.44
  311.3 2.1 copy-start.40
  311.3 2.1 copy-start.39
  374.6 2.9 copy-start.10
  380.3 4.5 %copy-start.28 = (f32[4,384]{1,0:T(4,128)S(1)}, f32[4,384]{1,0:T(4,128)}, u32[]{:S(2)}) copy-start(f32[4,384]{1,0:T(4,128)} %param.18) | copy-start | bytes 18436
  380.3 9.2 %collective-permute-start.1 = (f32[2,512,384]{2,1,0:T(8,128)}, f32[2,512,384]{2,1,0:T(8,128)}, u32[]{:S(2)}, u32[]{:S(2)}) collective-permute-start(f32[2,512,384]{2,1,0:T(8,128)} %maximum_select_fusion.2), channel_id=1, source_target_pairs={{0,1},{1,0},{2,3},{3,2},{4,5},{5,4},{6,7},{7,6},{8,9},{9,8},{10,11... | collective-permute-start | bytes 4718600 | tf_op jit(solution)/shard_map/ppermute | solution.py:510
  391.7 3.0 copy-start.15
  (1 other events, 0.6 us)
